TPU v7x, 32 devices: a whole 2x2x4 slice. The times are simulated.
32 devices in a mesh: team: 16 (over z, x, core), member: 2 (over y).
Axes of the slice: x: 2, y: 2, z: 4, core: 2. Of those that a mesh axis runs over, the one named last changes fastest.
Arguments:
- embeddings: float32 [16384, 256], P('team'), may hold values from -1 to 1, as said below
Outputs:
- forces: float32 [16384, 256], P(('team', 'member'))
Inputs may be any that keep to these rules, and one draw needn't show every extreme that they name: `embeddings`: every row has Euclidean length one.
All inputs are finite; a program needn't handle non-finite values.
Results may differ from a plain program's by a relative error of at most 0.00005.
Values sent between devices are 32-bit elements; how exact they have to be, the bound alone decides.
No kernel may reach another device: no remote copies, remote signals or barrier semaphores. Data moves between devices by JAX's collectives and lax.ppermute only.
A program may use at most 64 MiB of HBM per device.

v0:
```python
import jax
import jax.numpy as jnp
from jax import lax
from jax.sharding import PartitionSpec as P

CORES = 2
COLUMNS = 2


def moved(value, axis, target):
    count = lax.axis_size(axis)
    pairs = [(source, target(source)) for source in range(count)]
    return lax.ppermute(value, axis, [pair for pair in pairs if pair[1] is not None])


def core_swap(value):
    return moved(value, "team", lambda team: team ^ 1)


def column_swap(value):
    return moved(value, "team", lambda team: team ^ CORES)


def along_line(value, target):
    line = CORES * COLUMNS

    def team_target(team):
        layer = target(team // line)
        return None if layer is None else layer * line + team % line

    return moved(value, "team", team_target)


def line_parts(part):
    layers = lax.axis_size("team") // (CORES * COLUMNS)
    if layers != 4:
        parts = []
        for _ in range(layers - 1):
            part = along_line(part, lambda layer: (layer + layers - 1) % layers)
            parts.append(part)
        return parts
    middle = {1: 2, 2: 1}.get
    outward = {1: 0, 2: 3}.get
    layer_index = lax.axis_index("team") // (CORES * COLUMNS)
    inner = (layer_index == 1) | (layer_index == 2)
    near = along_line(part, lambda layer: layer ^ 1)
    across = along_line(part, middle)
    across_far = along_line(near, middle)
    second = jnp.where(inner, across, along_line(across, outward))
    third = jnp.where(inner, across_far, along_line(across_far, outward))
    return [near, second, third]


def over_members(part):
    members = lax.axis_size("member")
    return [
        moved(part, "member", lambda member, step=step: (member + step) % members)
        for step in range(1, members)
    ]


def sums(rows, partners):
    similarity = lax.dot_general(
        rows,
        partners,
        (((1,), (1,)), ((), ())),
        precision=lax.Precision.HIGH,
        preferred_element_type=jnp.float32,
    )
    weights = jnp.exp(2.0 * similarity - 2.0)
    return jnp.dot(weights, partners, precision=lax.Precision.HIGH, preferred_element_type=jnp.float32)


def local(embeddings):
    members = lax.axis_size("member")
    share = embeddings.shape[0] // members
    part = lax.dynamic_slice_in_dim(embeddings, lax.axis_index("member") * share, share)
    partners = [embeddings]
    for piece in line_parts(part):
        partners.append(piece)
        partners.extend(over_members(piece))
    beside = column_swap(part)
    own_rows = jnp.concatenate([part, core_swap(part)])
    beside_rows = jnp.concatenate([beside, core_swap(beside)])
    own_sums = sum(sums(own_rows, piece) for piece in partners)
    beside_sums = sum(sums(beside_rows, piece) for piece in partners)
    returned = column_swap(beside_sums[:share] + core_swap(beside_sums[share:]))
    return own_sums[:share] + core_swap(own_sums[share:]) + returned


def solution(mesh):
    return jax.shard_map(
        local,
        mesh=mesh,
        in_specs=(P("team", None),),
        out_specs=P(("team", "member"), None),
        check_vma=False,
    )
```

profile of v0, /device:TPU:0, one launch (start us, length us, event | category | flops | bytes accessed | tf_op | source)
XLA Modules:
  0.0 89.7 jit_solution(16536782780437583343)
XLA Ops:
  0.0 1.2 %copy-done = f32[1024,256]{1,0:T(8,128)S(1)} copy-done((f32[1024,256]{1,0:T(8,128)S(1)}, f32[1024,256]{1,0:T(8,128)}, u32[]{:S(2)}) %copy-start) | copy-done | bytes 1048600
  1.3 3.1 %collective-permute-start.1 = (f32[512,256]{1,0:T(8,128)S(1)}, f32[512,256]{1,0:T(8,128)S(1)}, u32[]{:S(2)}, u32[]{:S(2)}) collective-permute-start(f32[512,256]{1,0:T(8,128)S(1)} %constant_dynamic-slice_fusion), channel_id=1, source_target_pairs={{0,8},{2,10},{4,12},{6,14},{8,0},{10,2},{12,4},{14,6},{16,24},{18,... | collective-permute-start | bytes 1572872 | tf_op jit(solution)/shard_map/ppermute | solution.py:13
  5.1 1.6 %collective-permute-start.10 = (f32[512,256]{1,0:T(8,128)S(1)}, f32[512,256]{1,0:T(8,128)}, u32[]{:S(2)}, u32[]{:S(2)}) collective-permute-start(f32[512,256]{1,0:T(8,128)S(1)} %constant_dynamic-slice_fusion), channel_id=1, source_target_pairs={{0,4},{2,6},{4,0},{6,2},{8,12},{10,14},{12,8},{14,10},{16,20},{18,... | collective-permute-start | bytes 1572872 | tf_op jit(solution)/shard_map/ppermute | solution.py:13
  6.7 9.6 %collective-permute-done.1 = f32[512,256]{1,0:T(8,128)S(1)} collective-permute-done((f32[512,256]{1,0:T(8,128)S(1)}, f32[512,256]{1,0:T(8,128)S(1)}, u32[]{:S(2)}, u32[]{:S(2)}) %collective-permute-start.1) | collective-permute-done | bytes 524320 | tf_op jit(solution)/shard_map/ppermute | solution.py:13
  17.0 1.7 %collective-permute-start.2 = (f32[512,256]{1,0:T(8,128)S(1)}, f32[512,256]{1,0:T(8,128)S(1)}, u32[]{:S(2)}, u32[]{:S(2)}) collective-permute-start(f32[512,256]{1,0:T(8,128)S(1)} %collective-permute-done.1), channel_id=1, source_target_pairs={{0,1},{1,0},{2,3},{3,2},{4,5},{5,4},{6,7},{7,6},{8,9},{9,8},{10,11... | collective-permute-start | bytes 1572872 | tf_op jit(solution)/shard_map/ppermute | solution.py:13
  18.7 1.3 %collective-permute-start.4 = (f32[512,256]{1,0:T(8,128)S(1)}, f32[512,256]{1,0:T(8,128)S(1)}, u32[]{:S(2)}, u32[]{:S(2)}) collective-permute-start(f32[512,256]{1,0:T(8,128)S(1)} %collective-permute-done.3), channel_id=1, source_target_pairs={{8,0},{10,2},{12,4},{14,6},{16,24},{18,26},{20,28},{22,30},{9,1},{... | collective-permute-start | bytes 1572872 | tf_op jit(solution)/shard_map/ppermute | solution.py:13
  20.0 1.9 %fusion.155 = f32[1024,1024]{1,0:T(8,128)S(1)} fusion(f32[1024,256]{1,0:T(8,128)S(1)} %copy-done, f32[512,256]{1,0:T(8,128)S(1)} %collective-permute-done, f32[512,256]{1,0:T(8,128)S(1)} %constant_dynamic-slice_fusion), kind=kOutput, calls=%fused_computation.139 | convolution fusion | flops 1610874880 | bytes 6291456 | tf_op jit(solution)/shard_map/dot_general | solution.py:63
  22.0 2.1 %fusion.4 = f32[1024,256]{1,0:T(8,128)S(1)} fusion(f32[1024,256]{1,0:T(8,128)S(1)} %copy-done, f32[1024,1024]{1,0:T(8,128)S(1)} %fusion.155), kind=kOutput, calls=%fused_computation.4 | convolution fusion | flops 1612709888 | bytes 6291456 | tf_op jit(solution)/shard_map/dot_general | solution.py:71
  27.5 7.5 %collective-permute-done.4 = f32[512,256]{1,0:T(8,128)S(1)} collective-permute-done((f32[512,256]{1,0:T(8,128)S(1)}, f32[512,256]{1,0:T(8,128)S(1)}, u32[]{:S(2)}, u32[]{:S(2)}) %collective-permute-start.4) | collective-permute-done | bytes 524320 | tf_op jit(solution)/shard_map/ppermute | solution.py:13
  36.7 1.9 %fusion.156 = f32[1024,1024]{1,0:T(8,128)S(1)} fusion(f32[1024,256]{1,0:T(8,128)S(1)} %constant_dynamic-update-slice_fusion, f32[1024,256]{1,0:T(8,128)S(1)} %copy-done), kind=kOutput, calls=%fused_computation.140 | convolution fusion | flops 1610612736 | bytes 6291456 | tf_op jit(solution)/shard_map/dot_general | solution.py:63
  38.6 1.2 %fusion.20 = f32[1024,256]{1,0:T(8,128)S(1)} fusion(f32[512,256]{1,0:T(8,128)S(1)} %broadcast_select_fusion.1, f32[1024,512]{1,0:T(8,128)S(1)} %fusion.159), kind=kOutput, calls=%fused_computation.20 | convolution fusion | flops 806354944 | bytes 3670016 | tf_op jit(solution)/shard_map/dot_general | solution.py:71
  40.8 1.4 %fusion.44 = f32[1024,256]{1,0:T(8,128)S(1)} fusion(f32[512,256]{1,0:T(8,128)S(1)} %broadcast_select_fusion.1, f32[1024,512]{1,0:T(8,128)S(1)} %fusion.152), kind=kOutput, calls=%fused_computation.44 | convolution fusion | flops 806354944 | bytes 3670016 | tf_op jit(solution)/shard_map/dot_general | solution.py:71
  43.2 1.3 %collective-permute-start.7 = (f32[512,256]{1,0:T(8,128)S(1)}, f32[512,256]{1,0:T(8,128)S(1)}, u32[]{:S(2)}, u32[]{:S(2)}) collective-permute-start(f32[512,256]{1,0:T(8,128)S(1)} %collective-permute-done.6), channel_id=1, source_target_pairs={{8,0},{10,2},{12,4},{14,6},{16,24},{18,26},{20,28},{22,30},{9,1},{... | collective-permute-start | bytes 1572872 | tf_op jit(solution)/shard_map/ppermute | solution.py:13
  44.5 2.1 %fusion = f32[1024,256]{1,0:T(8,128)S(1)} fusion(f32[1024,256]{1,0:T(8,128)S(1)} %copy-done, f32[1024,1024]{1,0:T(8,128)S(1)} %fusion.156), kind=kOutput, calls=%fused_computation | convolution fusion | flops 1612709888 | bytes 6291456 | tf_op jit(solution)/shard_map/dot_general | solution.py:71
  49.9 6.6 %collective-permute-done.7 = f32[512,256]{1,0:T(8,128)S(1)} collective-permute-done((f32[512,256]{1,0:T(8,128)S(1)}, f32[512,256]{1,0:T(8,128)S(1)}, u32[]{:S(2)}, u32[]{:S(2)}) %collective-permute-start.7) | collective-permute-done | bytes 524320 | tf_op jit(solution)/shard_map/ppermute | solution.py:13
  56.6 1.6 %collective-permute-start.8 = (f32[512,256]{1,0:T(8,128)S(1)}, f32[512,256]{1,0:T(8,128)S(1)}, u32[]{:S(2)}, u32[]{:S(2)}) collective-permute-start(f32[512,256]{1,0:T(8,128)S(1)} %broadcast_select_fusion), channel_id=1, source_target_pairs={{0,1},{1,0},{2,3},{3,2},{4,5},{5,4},{6,7},{7,6},{8,9},{9,8},{10,11... | collective-permute-start | bytes 1572872 | tf_op jit(solution)/shard_map/ppermute | solution.py:13
  63.6 1.2 %fusion.87 = f32[1024,256]{1,0:T(8,128)S(1)} fusion(f32[1024,256]{1,0:T(8,128)S(1)} %fusion.16, f32[1024,256]{1,0:T(8,128)S(1)} %fusion.20, f32[1024,256]{1,0:T(8,128)S(1)} %fusion.78, f32[512,256]{1,0:T(8,128)S(1)} %collective-permute-done.2, f32[1024,512]{1,0:T(8,128)S(1)} %fusion.158), kind=kOutput, calls=%fused_computation.69 | convolution fusion | flops 807141376 | bytes 6815744 | tf_op jit(solution)/shard_map/dot_general | solution.py:71
  64.8 1.2 %fusion.150 = f32[1024,512]{1,0:T(8,128)S(1)} fusion(f32[512,256]{1,0:T(8,128)S(1)} %broadcast_select_fusion, f32[512,256]{1,0:T(8,128)S(1)} %collective-permute-done, f32[512,256]{1,0:T(8,128)S(1)} %constant_dynamic-slice_fusion), kind=kOutput, calls=%fused_computation.134 | convolution fusion | flops 805568512 | bytes 3670016 | tf_op jit(solution)/shard_map/dot_general | solution.py:63
  66.1 1.2 %fusion.69 = f32[1024,256]{1,0:T(8,128)S(1)} fusion(f32[1024,256]{1,0:T(8,128)S(1)} %fusion.40, f32[1024,256]{1,0:T(8,128)S(1)} %fusion.44, f32[1024,256]{1,0:T(8,128)S(1)} %fusion.60, f32[512,256]{1,0:T(8,128)S(1)} %collective-permute-done.2, f32[1024,512]{1,0:T(8,128)S(1)} %fusion.153), kind=kOutput, calls=%fused_computation.63 | convolution fusion | flops 807141376 | bytes 6815744 | tf_op jit(solution)/shard_map/dot_general | solution.py:71
  68.3 1.2 %fusion.8 = f32[1024,256]{1,0:T(8,128)S(1)} fusion(f32[512,256]{1,0:T(8,128)S(1)} %collective-permute-done.8, f32[1024,512]{1,0:T(8,128)S(1)} %fusion.162), kind=kOutput, calls=%fused_computation.8 | convolution fusion | flops 806354944 | bytes 3670016 | tf_op jit(solution)/shard_map/dot_general | solution.py:71
  69.5 1.2 %fusion.93 = f32[1024,256]{1,0:T(8,128)S(1)} fusion(f32[1024,256]{1,0:T(8,128)S(1)} %fusion.8, f32[1024,256]{1,0:T(8,128)S(1)} %fusion.87, f32[512,256]{1,0:T(8,128)S(1)} %broadcast_select_fusion, f32[1024,512]{1,0:T(8,128)S(1)} %fusion.161), kind=kOutput, calls=%fused_computation.71 | convolution fusion | flops 806879232 | bytes 5767168 | tf_op jit(solution)/shard_map/dot_general | solution.py:71
  73.0 1.2 %fusion.75 = f32[1024,256]{1,0:T(8,128)S(1)} fusion(f32[1024,256]{1,0:T(8,128)S(1)} %fusion.32, f32[1024,256]{1,0:T(8,128)S(1)} %fusion.69, f32[512,256]{1,0:T(8,128)S(1)} %broadcast_select_fusion, f32[1024,512]{1,0:T(8,128)S(1)} %fusion.150), kind=kOutput, calls=%fused_computation.65 | convolution fusion | flops 806879232 | bytes 5767168 | tf_op jit(solution)/shard_map/dot_general | solution.py:71
  74.9 1.6 %collective-permute-start.13 = (f32[512,256]{1,0:T(8,128)S(1)}, f32[512,256]{1,0:T(8,128)S(1)}, u32[]{:S(2)}, u32[]{:S(2)}) collective-permute-start(f32[512,256]{1,0:T(8,128)S(1)} %slice_add_fusion), channel_id=1, source_target_pairs={{0,4},{2,6},{4,0},{6,2},{8,12},{10,14},{12,8},{14,10},{16,20},{18,... | collective-permute-start | bytes 1572872 | tf_op jit(solution)/shard_map/ppermute | solution.py:13
  76.5 12.4 %collective-permute-done.13 = f32[512,256]{1,0:T(8,128)S(1)} collective-permute-done((f32[512,256]{1,0:T(8,128)S(1)}, f32[512,256]{1,0:T(8,128)S(1)}, u32[]{:S(2)}, u32[]{:S(2)}) %collective-permute-start.13) | collective-permute-done | bytes 524320 | tf_op jit(solution)/shard_map/ppermute | solution.py:13
  (43 shorter events, 22.1 us)
Async XLA Ops:
  0.0 1.2 %copy-start = (f32[1024,256]{1,0:T(8,128)S(1)}, f32[1024,256]{1,0:T(8,128)}, u32[]{:S(2)}) copy-start(f32[1024,256]{1,0:T(8,128)} %param.1) | copy-start | bytes 3145732
  1.3 15.0 %collective-permute-start.1 = (f32[512,256]{1,0:T(8,128)S(1)}, f32[512,256]{1,0:T(8,128)S(1)}, u32[]{:S(2)}, u32[]{:S(2)}) collective-permute-start(f32[512,256]{1,0:T(8,128)S(1)} %constant_dynamic-slice_fusion), channel_id=1, source_target_pairs={{0,8},{2,10},{4,12},{6,14},{8,0},{10,2},{12,4},{14,6},{16,24},{18,... | collective-permute-start | bytes 1572872 | tf_op jit(solution)/shard_map/ppermute | solution.py:13
  4.4 14.4 %collective-permute-start.3 = (f32[512,256]{1,0:T(8,128)S(1)}, f32[512,256]{1,0:T(8,128)S(1)}, u32[]{:S(2)}, u32[]{:S(2)}) collective-permute-start(f32[512,256]{1,0:T(8,128)S(1)} %constant_dynamic-slice_fusion), channel_id=1, source_target_pairs={{8,16},{10,18},{12,20},{14,22},{16,8},{18,10},{20,12},{22,14},{9,1... | collective-permute-start | bytes 1572872 | tf_op jit(solution)/shard_map/ppermute | solution.py:13
  5.0 15.0 %collective-permute-start = (f32[512,256]{1,0:T(8,128)S(1)}, f32[512,256]{1,0:T(8,128)S(1)}, u32[]{:S(2)}, u32[]{:S(2)}) collective-permute-start(f32[512,256]{1,0:T(8,128)S(1)} %constant_dynamic-slice_fusion), channel_id=1, source_target_pairs={{0,2},{2,0},{4,6},{6,4},{8,10},{10,8},{12,14},{14,12},{16,18},{18,... | collective-permute-start | bytes 1572872 | tf_op jit(solution)/shard_map/ppermute | solution.py:13
  5.1 20.0 %collective-permute-start.10 = (f32[512,256]{1,0:T(8,128)S(1)}, f32[512,256]{1,0:T(8,128)}, u32[]{:S(2)}, u32[]{:S(2)}) collective-permute-start(f32[512,256]{1,0:T(8,128)S(1)} %constant_dynamic-slice_fusion), channel_id=1, source_target_pairs={{0,4},{2,6},{4,0},{6,2},{8,12},{10,14},{12,8},{14,10},{16,20},{18,... | collective-permute-start | bytes 1572872 | tf_op jit(solution)/shard_map/ppermute | solution.py:13
  16.3 26.9 %collective-permute-start.6 = (f32[512,256]{1,0:T(8,128)S(1)}, f32[512,256]{1,0:T(8,128)S(1)}, u32[]{:S(2)}, u32[]{:S(2)}) collective-permute-start(f32[512,256]{1,0:T(8,128)S(1)} %collective-permute-done.1), channel_id=1, source_target_pairs={{8,16},{10,18},{12,20},{14,22},{16,8},{18,10},{20,12},{22,14},{9,1... | collective-permute-start | bytes 1572872 | tf_op jit(solution)/shard_map/ppermute | solution.py:13
  17.0 29.7 %collective-permute-start.2 = (f32[512,256]{1,0:T(8,128)S(1)}, f32[512,256]{1,0:T(8,128)S(1)}, u32[]{:S(2)}, u32[]{:S(2)}) collective-permute-start(f32[512,256]{1,0:T(8,128)S(1)} %collective-permute-done.1), channel_id=1, source_target_pairs={{0,1},{1,0},{2,3},{3,2},{4,5},{5,4},{6,7},{7,6},{8,9},{9,8},{10,11... | collective-permute-start | bytes 1572872 | tf_op jit(solution)/shard_map/ppermute | solution.py:13
  18.7 16.2 %collective-permute-start.4 = (f32[512,256]{1,0:T(8,128)S(1)}, f32[512,256]{1,0:T(8,128)S(1)}, u32[]{:S(2)}, u32[]{:S(2)}) collective-permute-start(f32[512,256]{1,0:T(8,128)S(1)} %collective-permute-done.3), channel_id=1, source_target_pairs={{8,0},{10,2},{12,4},{14,6},{16,24},{18,26},{20,28},{22,30},{9,1},{... | collective-permute-start | bytes 1572872 | tf_op jit(solution)/shard_map/ppermute | solution.py:13
  25.2 10.4 %collective-permute-start.11 = (f32[512,256]{1,0:T(8,128)}, f32[512,256]{1,0:T(8,128)S(1)}, u32[]{:S(2)}, u32[]{:S(2)}) collective-permute-start(f32[512,256]{1,0:T(8,128)} %collective-permute-done.10), channel_id=1, source_target_pairs={{0,2},{2,0},{4,6},{6,4},{8,10},{10,8},{12,14},{14,12},{16,18},{18,... | collective-permute-start | bytes 1572872 | tf_op jit(solution)/shard_map/ppermute | solution.py:13
  35.0 24.2 %collective-permute-start.5 = (f32[512,256]{1,0:T(8,128)S(1)}, f32[512,256]{1,0:T(8,128)S(1)}, u32[]{:S(2)}, u32[]{:S(2)}) collective-permute-start(f32[512,256]{1,0:T(8,128)S(1)} %broadcast_select_fusion.1), channel_id=1, source_target_pairs={{0,1},{1,0},{2,3},{3,2},{4,5},{5,4},{6,7},{7,6},{8,9},{9,8},{10,11... | collective-permute-start | bytes 1572872 | tf_op jit(solution)/shard_map/ppermute | solution.py:13
  43.2 13.3 %collective-permute-start.7 = (f32[512,256]{1,0:T(8,128)S(1)}, f32[512,256]{1,0:T(8,128)S(1)}, u32[]{:S(2)}, u32[]{:S(2)}) collective-permute-start(f32[512,256]{1,0:T(8,128)S(1)} %collective-permute-done.6), channel_id=1, source_target_pairs={{8,0},{10,2},{12,4},{14,6},{16,24},{18,26},{20,28},{22,30},{9,1},{... | collective-permute-start | bytes 1572872 | tf_op jit(solution)/shard_map/ppermute | solution.py:13
  56.6 10.7 %collective-permute-start.8 = (f32[512,256]{1,0:T(8,128)S(1)}, f32[512,256]{1,0:T(8,128)S(1)}, u32[]{:S(2)}, u32[]{:S(2)}) collective-permute-start(f32[512,256]{1,0:T(8,128)S(1)} %broadcast_select_fusion), channel_id=1, source_target_pairs={{0,1},{1,0},{2,3},{3,2},{4,5},{5,4},{6,7},{7,6},{8,9},{9,8},{10,11... | collective-permute-start | bytes 1572872 | tf_op jit(solution)/shard_map/ppermute | solution.py:13
  70.8 4.1 %collective-permute-start.12 = (f32[512,256]{1,0:T(8,128)S(1)}, f32[512,256]{1,0:T(8,128)S(1)}, u32[]{:S(2)}, u32[]{:S(2)}) collective-permute-start(f32[512,256]{1,0:T(8,128)S(1)} %slice.19), channel_id=1, source_target_pairs={{0,2},{2,0},{4,6},{6,4},{8,10},{10,8},{12,14},{14,12},{16,18},{18,... | collective-permute-start | bytes 1572872 | tf_op jit(solution)/shard_map/ppermute | solution.py:13
  74.3 2.2 %collective-permute-start.9 = (f32[512,256]{1,0:T(8,128)S(1)}, f32[512,256]{1,0:T(8,128)S(1)}, u32[]{:S(2)}, u32[]{:S(2)}) collective-permute-start(f32[512,256]{1,0:T(8,128)S(1)} %slice.17), channel_id=1, source_target_pairs={{0,2},{2,0},{4,6},{6,4},{8,10},{10,8},{12,14},{14,12},{16,18},{18,... | collective-permute-start | bytes 1572872 | tf_op jit(solution)/shard_map/ppermute | solution.py:13
  74.9 13.9 %collective-permute-start.13 = (f32[512,256]{1,0:T(8,128)S(1)}, f32[512,256]{1,0:T(8,128)S(1)}, u32[]{:S(2)}, u32[]{:S(2)}) collective-permute-start(f32[512,256]{1,0:T(8,128)S(1)} %slice_add_fusion), channel_id=1, source_target_pairs={{0,4},{2,6},{4,0},{6,2},{8,12},{10,14},{12,8},{14,10},{16,20},{18,... | collective-permute-start | bytes 1572872 | tf_op jit(solution)/shard_map/ppermute | solution.py:13
where the time goes:
time: 90 us; the launch traced here: 89.7 us
  waiting for transfers between devices  36.1 us (40%)
  matrix products  34.9 us (39%)
  starting transfers between devices  14.8 us (16%)
  local copies, waits for them, and re-layouts  2.44 us (3%)
  other arithmetic  1.1 us (1%)
    ppermute x14, waiting for transfers between devices, moved(): lax.ppermute(value, axis, [pair for pair in pairs if pair[1] is not None])  36.1 us
    dot_general x14, matrix products, sums(): jnp.dot(weights, partners, precision=lax.Precision.HIGH, preferred_elemen...  18.5 us
    dot_general x14, matrix products, sums(): lax.dot_general(rows, partners, (((1,), (1,)), ((), ())), precision=lax.P...  16.4 us
    ppermute x14, starting transfers between devices, moved(): lax.ppermute(value, axis, [pair for pair in pairs if pair[1] is not None])  14.8 us
    unnamed x3, local copies, waits for them, and re-layouts  2.3 us
  transfers between devices with their start and end apart: 14, of which 4 were waited for; matrix products, arithmetic and copies ran while one was open for 37% of the time, Pallas kernels for 0%

commit v1 on v0

--- a/solution.py
+++ b/solution.py
@@ -1,6 +1,11 @@
+import functools
+import math
+
 import jax
 import jax.numpy as jnp
 from jax import lax
+from jax.experimental import pallas as pl
+from jax.experimental.pallas import tpu as pltpu
 from jax.sharding import PartitionSpec as P
 
 CORES = 2
@@ -29,26 +34,6 @@
         return None if layer is None else layer * line + team % line
 
     return moved(value, "team", team_target)
-
-
-def line_parts(part):
-    layers = lax.axis_size("team") // (CORES * COLUMNS)
-    if layers != 4:
-        parts = []
-        for _ in range(layers - 1):
-            part = along_line(part, lambda layer: (layer + layers - 1) % layers)
-            parts.append(part)
-        return parts
-    middle = {1: 2, 2: 1}.get
-    outward = {1: 0, 2: 3}.get
-    layer_index = lax.axis_index("team") // (CORES * COLUMNS)
-    inner = (layer_index == 1) | (layer_index == 2)
-    near = along_line(part, lambda layer: layer ^ 1)
-    across = along_line(part, middle)
-    across_far = along_line(near, middle)
-    second = jnp.where(inner, across, along_line(across, outward))
-    third = jnp.where(inner, across_far, along_line(across_far, outward))
-    return [near, second, third]
 
 
 def over_members(part):
@@ -71,12 +56,15 @@
     return jnp.dot(weights, partners, precision=lax.Precision.HIGH, preferred_element_type=jnp.float32)
 
 
-def local(embeddings):
+def plain(embeddings):
     members = lax.axis_size("member")
+    layers = lax.axis_size("team") // (CORES * COLUMNS)
     share = embeddings.shape[0] // members
     part = lax.dynamic_slice_in_dim(embeddings, lax.axis_index("member") * share, share)
     partners = [embeddings]
-    for piece in line_parts(part):
+    piece = part
+    for _ in range(layers - 1):
+        piece = along_line(piece, lambda layer: (layer + layers - 1) % layers)
         partners.append(piece)
         partners.extend(over_members(piece))
     beside = column_swap(part)
@@ -88,6 +76,160 @@
     return own_sums[:share] + core_swap(own_sums[share:]) + returned
 
 
+ROW_TILE = 256
+PARTNER_TILE = 1024
+VMEM_ONLY = pl.BlockSpec(memory_space=pltpu.VMEM)
+NO_COST = pl.CostEstimate(flops=1, bytes_accessed=1, transcendentals=0)
+
+
+def split_terms(values):
+    high = values.astype(jnp.bfloat16)
+    return high, (values - high.astype(jnp.float32)).astype(jnp.bfloat16)
+
+
+def sums_kernel(*refs, jobs, n_pieces):
+    def take(count):
+        nonlocal refs
+        taken, refs = refs[:count], refs[count:]
+        return taken
+
+    pieces = take(n_pieces)
+    rows = [take(n_rows) for n_rows, _, _, _ in jobs]
+    totals = [take(n_rows if given else 0) for n_rows, given, _, _ in jobs]
+    outs = [take(n_rows) for n_rows, _, _, _ in jobs]
+    terms = [[take(2) for _ in range(n_rows)] for n_rows, _, _, _ in jobs]
+    partner_high, partner_low = refs
+    place = 0
+    for piece in pieces:
+        span = slice(place, place + piece.shape[0])
+        partner_high[span, :], partner_low[span, :] = split_terms(piece[...])
+        place += piece.shape[0]
+    for sources, targets in zip(rows, terms):
+        for source, (high, low) in zip(sources, targets):
+            high[...], low[...] = split_terms(source[...] * (2.0 / math.log(2.0)))
+    for job, (n_rows, given, start, length) in enumerate(jobs):
+        for first in range(0, length, PARTNER_TILE):
+            span = slice(start + first, start + min(first + PARTNER_TILE, length))
+            high, low = partner_high[span, :], partner_low[span, :]
+            keys = jnp.concatenate([high, low, high], axis=1)
+            values = jnp.concatenate([high, high, low], axis=0)
+            for number in range(n_rows):
+                row_high, row_low = terms[job][number]
+                out = outs[job][number]
+                for row in range(0, out.shape[0], ROW_TILE):
+                    tile = slice(row, row + ROW_TILE)
+                    similarity = lax.dot_general(
+                        jnp.concatenate([row_high[tile, :], row_high[tile, :], row_low[tile, :]], axis=1),
+                        keys,
+                        (((1,), (1,)), ((), ())),
+                        preferred_element_type=jnp.float32,
+                    )
+                    weight_high, weight_low = split_terms(jnp.exp2(similarity))
+                    added = jnp.dot(
+                        jnp.concatenate([weight_high, weight_low, weight_high], axis=1),
+                        values,
+                        preferred_element_type=jnp.float32,
+                    )
+                    if first:
+                        added = out[tile, :] + added
+                    elif given:
+                        added = totals[job][number][tile, :] + added
+                    out[tile, :] = added
+
+
+def add_sums(pieces, *jobs):
+    lengths = [piece.shape[0] for piece in pieces]
+    width = pieces[0].shape[1]
+    plan = tuple(
+        (len(rows), totals is not None, sum(lengths[:first]), sum(lengths[first:last]))
+        for totals, rows, first, last in jobs
+    )
+    rows = [part for job in jobs for part in job[1]]
+    operands = [*pieces, *rows, *[part for job in jobs for part in job[0] or ()]]
+    scratch = [pltpu.VMEM(part.shape, jnp.bfloat16) for part in rows for _ in range(2)]
+    scratch += [pltpu.VMEM((sum(lengths), width), jnp.bfloat16)] * 2
+    outs = pl.pallas_call(
+        functools.partial(sums_kernel, jobs=plan, n_pieces=len(pieces)),
+        out_shape=[jax.ShapeDtypeStruct(part.shape, jnp.float32) for part in rows],
+        in_specs=[VMEM_ONLY] * len(operands),
+        out_specs=[VMEM_ONLY] * len(rows),
+        scratch_shapes=scratch,
+        compiler_params=pltpu.CompilerParams(vmem_limit_bytes=32 << 20),
+        cost_estimate=NO_COST,
+    )(*operands)
+    grouped = []
+    for _, part_rows, _, _ in jobs:
+        grouped.append(list(outs[: len(part_rows)]))
+        outs = outs[len(part_rows) :]
+    return grouped
+
+
+def core_swap_parts(value):
+    return jnp.concatenate([core_swap(rows) for rows in jnp.split(value, 2)])
+
+
+def half(block, index):
+    share = block.shape[0] // 2
+    return lax.dynamic_slice_in_dim(block, index * share, share)
+
+
+def staged(embeddings):
+    share = embeddings.shape[0] // 2
+    stage = lax.optimization_barrier
+    member = lax.axis_index("member")
+    layer_index = lax.axis_index("team") // (CORES * COLUMNS)
+    inner = (layer_index == 1) | (layer_index == 2)
+
+    part = half(embeddings, member)
+    near = along_line(part, lambda layer: layer ^ 1)
+    second = along_line(part, lambda layer: 3 - layer)
+    block_swapped = core_swap(embeddings)
+    beside = column_swap(part)
+    own = [part, half(block_swapped, member)]
+    other = [half(embeddings, 1 - member), half(block_swapped, 1 - member)]
+    (own_sums,) = add_sums([embeddings], (None, own, 0, 1))
+    own_sums, beside = stage((own_sums, beside))
+    far = [beside, core_swap_parts(beside)]
+    (far_sums,) = add_sums([embeddings], (None, far, 0, 1))
+
+    far_sums, second, near = stage((far_sums, second, near))
+    third = along_line(jnp.where(inner, second, part), {0: 2, 1: 0, 2: 3, 3: 1}.get)
+    near_beside = column_swap(near)
+    (second_over,) = over_members(second)
+    other_sums, far_sums, own_sums = add_sums(
+        [near, second], (None, other, 0, 1), (far_sums, far, 1, 2), (own_sums, own, 0, 2)
+    )
+
+    own_sums, far_sums, other_sums, third = stage((own_sums, far_sums, other_sums, third))
+    first_half, second_half = third[: share // 2], third[share // 2 :]
+    (third_over,) = over_members(first_half)
+    third_beside = column_swap(second_half)
+    other_sums, far_sums = add_sums(
+        [near_beside, second_half, first_half, second_over], (other_sums, other, 0, 2), (far_sums, far, 2, 4)
+    )
+
+    third_over, third_beside, own_sums, far_sums, other_sums = stage(
+        (third_over, third_beside, own_sums, far_sums, other_sums)
+    )
+    far_sums, other_sums = add_sums(
+        [third_over, third_beside], (far_sums, far, 0, 1), (other_sums, other, 1, 2)
+    )
+    far_total = far_sums[0] + core_swap(far_sums[1])
+    other_total = other_sums[0] + core_swap(other_sums[1])
+
+    far_total, other_total, own_sums = stage((far_total, other_total, own_sums))
+    far_returned = column_swap(far_total)
+    (other_returned,) = over_members(other_total)
+    (own_sums,) = add_sums([near_beside, second_over, third, third_over, third_beside], (own_sums, own, 0, 5))
+    swapped = core_swap_parts(own_sums[1])
+    return (own_sums[0] + swapped + far_returned + other_returned) * math.exp(-2.0)
+
+
+def local(embeddings):
+    layers = lax.axis_size("team") // (CORES * COLUMNS)
+    return (staged if layers == 4 and lax.axis_size("member") == 2 else plain)(embeddings)
+
+
 def solution(mesh):
     return jax.shard_map(
         local,

time: 90 us -> 75.9 us (0.84)
  matrix products: 34.9 us -> 0 us
  Pallas kernels: 0 us -> 32.4 us
  waiting for transfers between devices: 36.1 us -> 19.9 us
  local copies, waits for them, and re-layouts: 2.44 us -> 5.15 us
  starting transfers between devices: 14.8 us -> 16.9 us
    dot_general x28 -> x0, matrix products: 34.9 us -> none  [the longest x14 18.5 us: sums(): jnp.dot(weights, partners, precision=lax.Precision.HIGH, preferred_elemen...]
    pallas_call x0 -> x6, Pallas kernels: none -> 32.4 us  [add_sums(): pl.pallas_call(functools.partial(sums_kernel, jobs=plan, n_pieces=len(pie...]
    ppermute x14 -> x17, waiting for transfers between devices: 36.1 us -> 19.9 us  [moved(): lax.ppermute(value, axis, [pair for pair in pairs if pair[1] is not None])]
    dynamic_slice x1 -> x2, local copies, waits for them, and re-layouts: 0.03 us -> 3.33 us  [half(): return lax.dynamic_slice_in_dim(block, index * share, share)]
    ppermute x14 -> x17, starting transfers between devices: 14.8 us -> 16.9 us  [moved(): lax.ppermute(value, axis, [pair for pair in pairs if pair[1] is not None])]
    unnamed x3 -> x17, local copies, waits for them, and re-layouts: 2.3 us -> 1 us
    mul x0 -> x1, other arithmetic: none -> 0.93 us  [staged(): (own_sums[0] + swapped + far_returned + other_returned) * math.exp(-2.0)]
  transfers between devices with their start and end apart: 14 -> 17, of which waited for: 4 -> 10; matrix products, arithmetic and copies ran while one was open for 37% -> 7% of each run, Pallas kernels for 0% -> 40%
where the time goes in v1:
time: 75.9 us; the launch traced here: 75.6 us
  Pallas kernels  32.4 us (43%)
  waiting for transfers between devices  19.9 us (26%)
  starting transfers between devices  16.9 us (22%)
  local copies, waits for them, and re-layouts  5.15 us (7%)
  other arithmetic  1.13 us (1%)
    pallas_call x6, Pallas kernels, add_sums(): pl.pallas_call(functools.partial(sums_kernel, jobs=plan, n_pieces=len(pie...  32.4 us
    ppermute x17, waiting for transfers between devices, moved(): lax.ppermute(value, axis, [pair for pair in pairs if pair[1] is not None])  19.9 us
    ppermute x17, starting transfers between devices, moved(): lax.ppermute(value, axis, [pair for pair in pairs if pair[1] is not None])  16.9 us
    dynamic_slice x2, local copies, waits for them, and re-layouts, half(): return lax.dynamic_slice_in_dim(block, index * share, share)  3.33 us
  transfers between devices with their start and end apart: 17, of which 10 were waited for; matrix products, arithmetic and copies ran while one was open for 7% of the time, Pallas kernels for 40%

profile of v1, /device:TPU:0, one launch (start us, length us, event | category | flops | bytes accessed | tf_op | source)
XLA Modules:
  0.0 75.6 jit_solution(15942440941301142836)
XLA Ops:
  0.5 1.3 %constant_dynamic-slice_fusion.1 = (f32[512,256]{1,0:T(8,128)S(1)}, f32[512,256]{1,0:T(8,128)S(1)}) fusion(f32[1024,256]{1,0:T(8,128)} %refs_0_.3, s32[]{:T(128)S(6)} %select_n.22, s32[]{:T(128)S(6)} %select_n.21), kind=kLoop, calls=%fused_computation.8 | loop fusion | bytes 2097160 | tf_op jit(solution)/shard_map/dynamic_slice | solution.py:173
  1.7 2.6 %collective-permute-start.1 = (f32[512,256]{1,0:T(8,128)S(1)}, f32[512,256]{1,0:T(8,128)S(1)}, u32[]{:S(2)}, u32[]{:S(2)}) collective-permute-start(f32[512,256]{1,0:T(8,128)S(1)} %get-tuple-element.100.refs_1_.refs_6_.refs_5_), channel_id=1, source_target_pairs={{0,4},{2,6},{4,0},{6,2},{8,12},{10,14},{12,8},{14,10},{16,20},{18,... | collective-permute-start | bytes 1572872 | tf_op jit(solution)/shard_map/ppermute | solution.py:18
  4.3 3.6 %collective-permute-start.4 = (f32[512,256]{1,0:T(8,128)S(1)}, f32[512,256]{1,0:T(8,128)}, u32[]{:S(2)}, u32[]{:S(2)}) collective-permute-start(f32[512,256]{1,0:T(8,128)S(1)} %get-tuple-element.100.refs_1_.refs_6_.refs_5_), channel_id=1, source_target_pairs={{0,24},{2,26},{4,28},{6,30},{8,16},{10,18},{12,20},{14,22},{16,8},... | collective-permute-start | bytes 1572872 | tf_op jit(solution)/shard_map/ppermute | solution.py:18
  7.9 2.1 %constant_dynamic-slice_fusion = (f32[512,256]{1,0:T(8,128)}, f32[512,256]{1,0:T(8,128)S(1)}) fusion(f32[1024,256]{1,0:T(8,128)} %collective-permute-done, s32[]{:T(128)S(6)} %select_n.22, s32[]{:T(128)S(6)} %select_n.21), kind=kLoop, calls=%fused_computation.7 | loop fusion | bytes 2097160 | tf_op jit(solution)/shard_map/dynamic_slice | solution.py:173
  10.0 4.1 %shard_map.17 = (f32[512,256]{1,0:T(8,128)S(1)}, f32[512,256]{1,0:T(8,128)S(1)}) custom-call(f32[1024,256]{1,0:T(8,128)S(1)} %copy-done, f32[512,256]{1,0:T(8,128)S(1)} %get-tuple-element.100.refs_1_.refs_6_.refs_5_, f32[512,256]{1,0:T(8,128)S(1)} %get-tuple-element.98.refs_2_.refs_7_.refs_6_), custom_call_target="tpu_custom_call" | custom-call | flops 1 | bytes 1 | tf_op jit(solution)/shard_map/pallas_call | solution.py:151
  14.1 2.8 %collective-permute-done.1.refs_1_.refs_4_.refs_6_.refs_2_ = f32[512,256]{1,0:T(8,128)S(1)} collective-permute-done((f32[512,256]{1,0:T(8,128)S(1)}, f32[512,256]{1,0:T(8,128)S(1)}, u32[]{:S(2)}, u32[]{:S(2)}) %collective-permute-start.1) | collective-permute-done | bytes 524320 | tf_op jit(solution)/shard_map/ppermute | solution.py:18
  18.1 1.2 %collective-permute-done.2 = f32[256,256]{1,0:T(8,128)} collective-permute-done((f32[256,256]{1,0:T(8,128)S(1)}, f32[256,256]{1,0:T(8,128)}, u32[]{:S(2)}, u32[]{:S(2)}) %collective-permute-start.2) | collective-permute-done | bytes 262176 | tf_op jit(solution)/shard_map/ppermute | solution.py:18
  19.3 1.0 %constant_dynamic-update-slice_fusion.1 = f32[512,256]{1,0:T(8,128)S(1)} fusion(f32[256,256]{1,0:T(8,128)} %collective-permute-done.2), kind=kLoop, calls=%fused_computation.6 | loop fusion | bytes 524288
  20.3 4.1 %shard_map.18 = (f32[512,256]{1,0:T(8,128)S(1)}, f32[512,256]{1,0:T(8,128)S(1)}) custom-call(f32[1024,256]{1,0:T(8,128)S(1)} %copy-done, f32[512,256]{1,0:T(8,128)S(1)} %collective-permute-done.1.refs_1_.refs_4_.refs_6_.refs_2_, f32[512,256]{1,0:T(8,128)S(1)} %constant_dynamic-update-slice_fusion.refs_2_.refs_5_.refs_7_.refs_3_), custom_call_target="tpu_custom_call" | custom-call | flops 1 | bytes 1 | tf_op jit(solution)/shard_map/pallas_call | solution.py:151
  24.4 7.2 %collective-permute-done.5.refs_0_ = f32[512,256]{1,0:T(8,128)} collective-permute-done((f32[512,256]{1,0:T(8,128)S(1)}, f32[512,256]{1,0:T(8,128)}, u32[]{:S(2)}, u32[]{:S(2)}) %collective-permute-start.5) | collective-permute-done | bytes 524320 | tf_op jit(solution)/shard_map/ppermute | solution.py:18
  31.7 2.0 %collective-permute-start.8 = (f32[512,256]{1,0:T(8,128)S(1)}, f32[512,256]{1,0:T(8,128)S(1)}, u32[]{:S(2)}, u32[]{:S(2)}) collective-permute-start(f32[512,256]{1,0:T(8,128)S(1)} %broadcast_select_fusion), channel_id=1, source_target_pairs={{0,16},{2,18},{4,20},{6,22},{8,0},{10,2},{12,4},{14,6},{16,24},{18... | collective-permute-start | bytes 1572872 | tf_op jit(solution)/shard_map/ppermute | solution.py:18
  34.3 1.5 %collective-permute-start.7 = (f32[512,256]{1,0:T(8,128)}, f32[512,256]{1,0:T(8,128)S(1)}, u32[]{:S(2)}, u32[]{:S(2)}) collective-permute-start(f32[512,256]{1,0:T(8,128)} %collective-permute-done.4.refs_1_), channel_id=1, source_target_pairs={{0,1},{1,0},{2,3},{3,2},{4,5},{5,4},{6,7},{7,6},{8,9},{9,8},{10,11... | collective-permute-start | bytes 1572872 | tf_op jit(solution)/shard_map/ppermute | solution.py:18
  35.8 8.6 %shard_map.19 = (f32[512,256]{1,0:T(8,128)S(1)}, f32[512,256]{1,0:T(8,128)S(1)}, f32[512,256]{1,0:T(8,128)S(1)}, f32[512,256]{1,0:T(8,128)S(1)}, f32[512,256]{1,0:T(8,128)S(1)}, /*index=5*/f32[512,256]{1,0:T(8,128)S(1)}) custom-call(f32[512,256]{1,0:T(8,128)} %collective-permute-done.5.refs_0_, f32[512,256]{1,0:T(8,128)} %collective-permute-done.4.refs_1_, ...), custom_call_target="tpu_custom_call" | custom-call | flops 1 | bytes 1 | tf_op jit(solution)/shard_map/pallas_call | solution.py:151
  44.5 1.8 %collective-permute-done.8.refs_2_ = f32[512,256]{1,0:T(8,128)S(1)} collective-permute-done((f32[512,256]{1,0:T(8,128)S(1)}, f32[512,256]{1,0:T(8,128)S(1)}, u32[]{:S(2)}, u32[]{:S(2)}) %collective-permute-start.8) | collective-permute-done | bytes 524320 | tf_op jit(solution)/shard_map/ppermute | solution.py:18
  46.9 1.5 %collective-permute-start.9 = (f32[256,256]{1,0:T(8,128)S(1)}, f32[256,256]{1,0:T(8,128)S(1)}, u32[]{:S(2)}, u32[]{:S(2)}) collective-permute-start(f32[256,256]{1,0:T(8,128)S(1)} %get-tuple-element.104.refs_2_), channel_id=1, source_target_pairs={{0,1},{1,0},{2,3},{3,2},{4,5},{5,4},{6,7},{7,6},{8,9},{9,8},{10,11... | collective-permute-start | bytes 786440 | tf_op jit(solution)/shard_map/ppermute | solution.py:18
  48.5 5.8 %shard_map.20 = (f32[512,256]{1,0:T(8,128)S(1)}, f32[512,256]{1,0:T(8,128)S(1)}, f32[512,256]{1,0:T(8,128)S(1)}, f32[512,256]{1,0:T(8,128)S(1)}) custom-call(f32[512,256]{1,0:T(8,128)S(1)} %collective-permute-done.6.refs_0_, f32[256,256]{1,0:T(8,128)S(1)} %get-tuple-element.103.refs_1_, f32[256,256]{1,0:T(8,128)S(1)} %get-tuple-element.104.refs_2_, ...), custom_call_target="tpu_custom_call" | custom-call | flops 1 | bytes 1 | tf_op jit(solution)/shard_map/pallas_call | solution.py:151
  54.3 2.3 %shard_map.21 = (f32[512,256]{1,0:T(8,128)S(1)}, f32[512,256]{1,0:T(8,128)S(1)}, f32[512,256]{1,0:T(8,128)S(1)}, f32[512,256]{1,0:T(8,128)S(1)}) custom-call(f32[256,256]{1,0:T(8,128)S(1)} %collective-permute-done.9.refs_0_.refs_3_, f32[256,256]{1,0:T(8,128)S(1)} %collective-permute-done.10.refs_1_.refs_4_, ...), custom_call_target="tpu_custom_call" | custom-call | flops 1 | bytes 1 | tf_op jit(solution)/shard_map/pallas_call | solution.py:151
  57.3 1.4 %collective-permute-done.12 = f32[512,256]{1,0:T(8,128)S(1)} collective-permute-done((f32[512,256]{1,0:T(8,128)S(1)}, f32[512,256]{1,0:T(8,128)S(1)}, u32[]{:S(2)}, u32[]{:S(2)}) %collective-permute-start.12) | collective-permute-done | bytes 524320 | tf_op jit(solution)/shard_map/ppermute | solution.py:18
  59.5 1.6 %collective-permute-start.15 = (f32[512,256]{1,0:T(8,128)S(1)}, f32[512,256]{1,0:T(8,128)S(1)}, u32[]{:S(2)}, u32[]{:S(2)}) collective-permute-start(f32[512,256]{1,0:T(8,128)S(1)} %add.26), channel_id=1, source_target_pairs={{0,4},{2,6},{4,0},{6,2},{8,12},{10,14},{12,8},{14,10},{16,20},{18,... | collective-permute-start | bytes 1572872 | tf_op jit(solution)/shard_map/ppermute | solution.py:18
  61.9 7.4 %shard_map.22 = (f32[512,256]{1,0:T(8,128)S(1)}, f32[512,256]{1,0:T(8,128)S(1)}) custom-call(f32[512,256]{1,0:T(8,128)S(1)} %collective-permute-done.6.refs_0_, f32[512,256]{1,0:T(8,128)S(1)} %collective-permute-done.7.refs_3_.refs_1_, f32[512,256]{1,0:T(8,128)S(1)} %collective-permute-done.8.refs_2_, f32[256,256]{1,0:T(8,128)S(1)} %collective-permute-done.9.refs_0_.refs_3_, ...), custom_call_target="tpu_custom_call" | custom-call | flops 1 | bytes 1 | tf_op jit(solution)/shard_map/pallas_call | solution.py:151
  69.9 1.0 %collective-permute-done.13 = f32[256,256]{1,0:T(8,128)S(1)} collective-permute-done((f32[256,256]{1,0:T(8,128)S(1)}, f32[256,256]{1,0:T(8,128)S(1)}, u32[]{:S(2)}, u32[]{:S(2)}) %collective-permute-start.13) | collective-permute-done | bytes 262176 | tf_op jit(solution)/shard_map/ppermute | solution.py:18
  71.3 2.2 %collective-permute-done.15 = f32[512,256]{1,0:T(8,128)S(1)} collective-permute-done((f32[512,256]{1,0:T(8,128)S(1)}, f32[512,256]{1,0:T(8,128)S(1)}, u32[]{:S(2)}, u32[]{:S(2)}) %collective-permute-start.15) | collective-permute-done | bytes 524320 | tf_op jit(solution)/shard_map/ppermute | solution.py:18
  73.5 1.2 %collective-permute-done.16 = f32[512,256]{1,0:T(8,128)S(1)} collective-permute-done((f32[512,256]{1,0:T(8,128)S(1)}, f32[512,256]{1,0:T(8,128)S(1)}, u32[]{:S(2)}, u32[]{:S(2)}) %collective-permute-start.16) | collective-permute-done | bytes 524320 | tf_op jit(solution)/shard_map/ppermute | solution.py:18
  74.7 0.9 %fusion.2 = f32[512,256]{1,0:T(8,128)} fusion(f32[512,256]{1,0:T(8,128)S(1)} %collective-permute-done.16, f32[512,256]{1,0:T(8,128)S(1)} %collective-permute-done.15, f32[512,256]{1,0:T(8,128)S(1)} %get-tuple-element.93, f32[256,256]{1,0:T(8,128)S(1)} %collective-permute-done.14, f32[256,256]{1,0:T(8,128)S(1)} %collective-permute-done.13), kind=kLoop, calls=%fused_computation.3 | loop fusion | flops 655360 | bytes 2621440 | tf_op jit(solution)/shard_map/mul | solution.py:225
  (43 shorter events, 6.2 us)
Async XLA Ops:
  0.0 7.9 %collective-permute-start = (f32[1024,256]{1,0:T(8,128)}, f32[1024,256]{1,0:T(8,128)}, u32[]{:S(2)}, u32[]{:S(2)}) collective-permute-start(f32[1024,256]{1,0:T(8,128)} %refs_0_.3), channel_id=1, source_target_pairs={{0,2},{2,0},{4,6},{6,4},{8,10},{10,8},{12,14},{14,12},{16,18},{18,... | collective-permute-start | bytes 3145736 | tf_op jit(solution)/shard_map/ppermute | solution.py:18
  1.7 8.2 %copy-start = (f32[1024,256]{1,0:T(8,128)S(1)}, f32[1024,256]{1,0:T(8,128)}, u32[]{:S(2)}) copy-start(f32[1024,256]{1,0:T(8,128)} %refs_0_.3) | copy-start | bytes 3145732
  1.7 15.2 %collective-permute-start.1 = (f32[512,256]{1,0:T(8,128)S(1)}, f32[512,256]{1,0:T(8,128)S(1)}, u32[]{:S(2)}, u32[]{:S(2)}) collective-permute-start(f32[512,256]{1,0:T(8,128)S(1)} %get-tuple-element.100.refs_1_.refs_6_.refs_5_), channel_id=1, source_target_pairs={{0,4},{2,6},{4,0},{6,2},{8,12},{10,14},{12,8},{14,10},{16,20},{18,... | collective-permute-start | bytes 1572872 | tf_op jit(solution)/shard_map/ppermute | solution.py:18
  4.3 20.1 %collective-permute-start.4 = (f32[512,256]{1,0:T(8,128)S(1)}, f32[512,256]{1,0:T(8,128)}, u32[]{:S(2)}, u32[]{:S(2)}) collective-permute-start(f32[512,256]{1,0:T(8,128)S(1)} %get-tuple-element.100.refs_1_.refs_6_.refs_5_), channel_id=1, source_target_pairs={{0,24},{2,26},{4,28},{6,30},{8,16},{10,18},{12,20},{14,22},{16,8},... | collective-permute-start | bytes 1572872 | tf_op jit(solution)/shard_map/ppermute | solution.py:18
  7.9 23.8 %collective-permute-start.5 = (f32[512,256]{1,0:T(8,128)S(1)}, f32[512,256]{1,0:T(8,128)}, u32[]{:S(2)}, u32[]{:S(2)}) collective-permute-start(f32[512,256]{1,0:T(8,128)S(1)} %get-tuple-element.100.refs_1_.refs_6_.refs_5_), channel_id=1, source_target_pairs={{0,8},{2,10},{4,12},{6,14},{8,0},{10,2},{12,4},{14,6},{16,24},{18,... | collective-permute-start | bytes 1572872 | tf_op jit(solution)/shard_map/ppermute | solution.py:18
  10.0 4.1 %copy-start.2 = (f32[512,256]{1,0:T(8,128)}, f32[512,256]{1,0:T(8,128)S(1)}, u32[]{:S(2)}) copy-start(f32[512,256]{1,0:T(8,128)S(1)} %get-tuple-element.98.refs_2_.refs_7_.refs_6_) | copy-start | bytes 1572868
  14.1 3.5 %copy-start.4 = (f32[512,256]{1,0:T(8,128)}, f32[512,256]{1,0:T(8,128)S(1)}, u32[]{:S(2)}) copy-start(f32[512,256]{1,0:T(8,128)S(1)} %get-tuple-element.60.refs_10_) | copy-start | bytes 1572868
  17.6 1.7 %collective-permute-start.2 = (f32[256,256]{1,0:T(8,128)S(1)}, f32[256,256]{1,0:T(8,128)}, u32[]{:S(2)}, u32[]{:S(2)}) collective-permute-start(f32[256,256]{1,0:T(8,128)S(1)} %get-tuple-element.106), channel_id=1, source_target_pairs={{0,2},{2,0},{4,6},{6,4},{8,10},{10,8},{12,14},{14,12},{16,18},{18,... | collective-permute-start | bytes 786440 | tf_op jit(solution)/shard_map/ppermute | solution.py:18
  17.7 2.6 %collective-permute-start.3 = (f32[256,256]{1,0:T(8,128)}, f32[256,256]{1,0:T(8,128)S(1)}, u32[]{:S(2)}, u32[]{:S(2)}) collective-permute-start(f32[256,256]{1,0:T(8,128)} %get-tuple-element.105), channel_id=1, source_target_pairs={{0,2},{2,0},{4,6},{6,4},{8,10},{10,8},{12,14},{14,12},{16,18},{18,... | collective-permute-start | bytes 786440 | tf_op jit(solution)/shard_map/ppermute | solution.py:18
  20.3 15.5 %copy-start.7 = (f32[512,256]{1,0:T(8,128)S(1)}, f32[512,256]{1,0:T(8,128)}, u32[]{:S(2)}) copy-start(f32[512,256]{1,0:T(8,128)} %copy-done.6) | copy-start | bytes 1572868
  31.6 4.2 %copy-start.1 = (f32[512,256]{1,0:T(8,128)S(1)}, f32[512,256]{1,0:T(8,128)}, u32[]{:S(2)}) copy-start(f32[512,256]{1,0:T(8,128)} %get-tuple-element.97.refs_3_.refs_5_) | copy-start | bytes 1572868
  31.7 4.2 %copy-start.3 = (f32[512,256]{1,0:T(8,128)S(1)}, f32[512,256]{1,0:T(8,128)}, u32[]{:S(2)}) copy-start(f32[512,256]{1,0:T(8,128)} %copy-done.2) | copy-start | bytes 1572868
  31.7 4.2 %copy-start.5 = (f32[512,256]{1,0:T(8,128)S(1)}, f32[512,256]{1,0:T(8,128)}, u32[]{:S(2)}) copy-start(f32[512,256]{1,0:T(8,128)} %copy-done.4) | copy-start | bytes 1572868
  31.7 14.6 %collective-permute-start.8 = (f32[512,256]{1,0:T(8,128)S(1)}, f32[512,256]{1,0:T(8,128)S(1)}, u32[]{:S(2)}, u32[]{:S(2)}) collective-permute-start(f32[512,256]{1,0:T(8,128)S(1)} %broadcast_select_fusion), channel_id=1, source_target_pairs={{0,16},{2,18},{4,20},{6,22},{8,0},{10,2},{12,4},{14,6},{16,24},{18... | collective-permute-start | bytes 1572872 | tf_op jit(solution)/shard_map/ppermute | solution.py:18
  33.8 14.7 %collective-permute-start.6 = (f32[512,256]{1,0:T(8,128)}, f32[512,256]{1,0:T(8,128)S(1)}, u32[]{:S(2)}, u32[]{:S(2)}) collective-permute-start(f32[512,256]{1,0:T(8,128)} %collective-permute-done.5.refs_0_), channel_id=1, source_target_pairs={{0,4},{2,6},{4,0},{6,2},{8,12},{10,14},{12,8},{14,10},{16,20},{18,... | collective-permute-start | bytes 1572872 | tf_op jit(solution)/shard_map/ppermute | solution.py:18
  34.3 14.2 %collective-permute-start.7 = (f32[512,256]{1,0:T(8,128)}, f32[512,256]{1,0:T(8,128)S(1)}, u32[]{:S(2)}, u32[]{:S(2)}) collective-permute-start(f32[512,256]{1,0:T(8,128)} %collective-permute-done.4.refs_1_), channel_id=1, source_target_pairs={{0,1},{1,0},{2,3},{3,2},{4,5},{5,4},{6,7},{7,6},{8,9},{9,8},{10,11... | collective-permute-start | bytes 1572872 | tf_op jit(solution)/shard_map/ppermute | solution.py:18
  46.3 8.0 %collective-permute-start.10 = (f32[256,256]{1,0:T(8,128)S(1)}, f32[256,256]{1,0:T(8,128)S(1)}, u32[]{:S(2)}, u32[]{:S(2)}) collective-permute-start(f32[256,256]{1,0:T(8,128)S(1)} %get-tuple-element.103.refs_1_), channel_id=1, source_target_pairs={{0,4},{2,6},{4,0},{6,2},{8,12},{10,14},{12,8},{14,10},{16,20},{18,... | collective-permute-start | bytes 786440 | tf_op jit(solution)/shard_map/ppermute | solution.py:18
  46.9 7.4 %collective-permute-start.9 = (f32[256,256]{1,0:T(8,128)S(1)}, f32[256,256]{1,0:T(8,128)S(1)}, u32[]{:S(2)}, u32[]{:S(2)}) collective-permute-start(f32[256,256]{1,0:T(8,128)S(1)} %get-tuple-element.104.refs_2_), channel_id=1, source_target_pairs={{0,1},{1,0},{2,3},{3,2},{4,5},{5,4},{6,7},{7,6},{8,9},{9,8},{10,11... | collective-permute-start | bytes 786440 | tf_op jit(solution)/shard_map/ppermute | solution.py:18
  56.7 2.0 %collective-permute-start.12 = (f32[512,256]{1,0:T(8,128)S(1)}, f32[512,256]{1,0:T(8,128)S(1)}, u32[]{:S(2)}, u32[]{:S(2)}) collective-permute-start(f32[512,256]{1,0:T(8,128)S(1)} %get-tuple-element.88), channel_id=1, source_target_pairs={{0,2},{2,0},{4,6},{6,4},{8,10},{10,8},{12,14},{14,12},{16,18},{18,... | collective-permute-start | bytes 1572872 | tf_op jit(solution)/shard_map/ppermute | solution.py:18
  56.8 2.6 %collective-permute-start.11 = (f32[512,256]{1,0:T(8,128)S(1)}, f32[512,256]{1,0:T(8,128)S(1)}, u32[]{:S(2)}, u32[]{:S(2)}) collective-permute-start(f32[512,256]{1,0:T(8,128)S(1)} %get-tuple-element.86), channel_id=1, source_target_pairs={{0,2},{2,0},{4,6},{6,4},{8,10},{10,8},{12,14},{14,12},{16,18},{18,... | collective-permute-start | bytes 1572872 | tf_op jit(solution)/shard_map/ppermute | solution.py:18
  59.5 14.0 %collective-permute-start.15 = (f32[512,256]{1,0:T(8,128)S(1)}, f32[512,256]{1,0:T(8,128)S(1)}, u32[]{:S(2)}, u32[]{:S(2)}) collective-permute-start(f32[512,256]{1,0:T(8,128)S(1)} %add.26), channel_id=1, source_target_pairs={{0,4},{2,6},{4,0},{6,2},{8,12},{10,14},{12,8},{14,10},{16,20},{18,... | collective-permute-start | bytes 1572872 | tf_op jit(solution)/shard_map/ppermute | solution.py:18
  61.0 13.7 %collective-permute-start.16 = (f32[512,256]{1,0:T(8,128)S(1)}, f32[512,256]{1,0:T(8,128)S(1)}, u32[]{:S(2)}, u32[]{:S(2)}) collective-permute-start(f32[512,256]{1,0:T(8,128)S(1)} %add.27), channel_id=1, source_target_pairs={{0,1},{1,0},{2,3},{3,2},{4,5},{5,4},{6,7},{7,6},{8,9},{9,8},{10,11... | collective-permute-start | bytes 1572872 | tf_op jit(solution)/shard_map/ppermute | solution.py:18
  69.3 1.6 %collective-permute-start.13 = (f32[256,256]{1,0:T(8,128)S(1)}, f32[256,256]{1,0:T(8,128)S(1)}, u32[]{:S(2)}, u32[]{:S(2)}) collective-permute-start(f32[256,256]{1,0:T(8,128)S(1)} %get-tuple-element.101), channel_id=1, source_target_pairs={{0,2},{2,0},{4,6},{6,4},{8,10},{10,8},{12,14},{14,12},{16,18},{18,... | collective-permute-start | bytes 786440 | tf_op jit(solution)/shard_map/ppermute | solution.py:18
  69.4 1.9 %collective-permute-start.14 = (f32[256,256]{1,0:T(8,128)S(1)}, f32[256,256]{1,0:T(8,128)S(1)}, u32[]{:S(2)}, u32[]{:S(2)}) collective-permute-start(f32[256,256]{1,0:T(8,128)S(1)} %get-tuple-element.102), channel_id=1, source_target_pairs={{0,2},{2,0},{4,6},{6,4},{8,10},{10,8},{12,14},{14,12},{16,18},{18,... | collective-permute-start | bytes 786440 | tf_op jit(solution)/shard_map/ppermute | solution.py:18
  (1 other events, 3.5 us)

commit v2 on v1

--- a/solution.py
+++ b/solution.py
@@ -77,7 +77,7 @@
 
 
 ROW_TILE = 256
-PARTNER_TILE = 1024
+PARTNER_TILE = 512
 VMEM_ONLY = pl.BlockSpec(memory_space=pltpu.VMEM)
 NO_COST = pl.CostEstimate(flops=1, bytes_accessed=1, transcendentals=0)
 
@@ -164,13 +164,13 @@
     return grouped
 
 
-def core_swap_parts(value):
-    return jnp.concatenate([core_swap(rows) for rows in jnp.split(value, 2)])
-
-
 def half(block, index):
     share = block.shape[0] // 2
     return lax.dynamic_slice_in_dim(block, index * share, share)
+
+
+def core_swap_parts(value, parts):
+    return jnp.concatenate([core_swap(rows) for rows in jnp.split(value, parts)])
 
 
 def staged(embeddings):
@@ -183,46 +183,59 @@
     part = half(embeddings, member)
     near = along_line(part, lambda layer: layer ^ 1)
     second = along_line(part, lambda layer: 3 - layer)
+    beside = column_swap(part)
     block_swapped = core_swap(embeddings)
-    beside = column_swap(part)
-    own = [part, half(block_swapped, member)]
-    other = [half(embeddings, 1 - member), half(block_swapped, 1 - member)]
-    (own_sums,) = add_sums([embeddings], (None, own, 0, 1))
-    own_sums, beside = stage((own_sums, beside))
-    far = [beside, core_swap_parts(beside)]
-    (far_sums,) = add_sums([embeddings], (None, far, 0, 1))
-
-    far_sums, second, near = stage((far_sums, second, near))
+    own, far, other = [part], [beside], [half(embeddings, 1 - member)]
+    (own_sums,) = add_sums([embeddings, block_swapped], (None, own, 0, 2))
+
+    second, near, beside, own_sums = stage((second, near, beside, own_sums))
     third = along_line(jnp.where(inner, second, part), {0: 2, 1: 0, 2: 3, 3: 1}.get)
     near_beside = column_swap(near)
     (second_over,) = over_members(second)
-    other_sums, far_sums, own_sums = add_sums(
-        [near, second], (None, other, 0, 1), (far_sums, far, 1, 2), (own_sums, own, 0, 2)
+    near_swapped, second_swapped = core_swap(near), core_swap(second)
+    far = [beside]
+    far_sums, other_sums, own_sums = add_sums(
+        [embeddings, block_swapped, second, second_swapped, near, near_swapped],
+        (None, far, 0, 4),
+        (None, other, 4, 6),
+        (own_sums, own, 4, 6),
     )
 
     own_sums, far_sums, other_sums, third = stage((own_sums, far_sums, other_sums, third))
     first_half, second_half = third[: share // 2], third[share // 2 :]
     (third_over,) = over_members(first_half)
     third_beside = column_swap(second_half)
+    third_swapped = core_swap_parts(third, 1)
+    near_beside_swapped, second_over_swapped = core_swap_parts(near_beside, 1), core_swap_parts(second_over, 1)
     other_sums, far_sums = add_sums(
-        [near_beside, second_half, first_half, second_over], (other_sums, other, 0, 2), (far_sums, far, 2, 4)
-    )
-
-    third_over, third_beside, own_sums, far_sums, other_sums = stage(
-        (third_over, third_beside, own_sums, far_sums, other_sums)
-    )
+        [
+            near_beside,
+            near_beside_swapped,
+            second_half,
+            third_swapped[share // 2 :],
+            first_half,
+            third_swapped[: share // 2],
+            second_over,
+            second_over_swapped,
+        ],
+        (other_sums, other, 0, 4),
+        (far_sums, far, 4, 8),
+    )
+
+    own_sums, far_sums, other_sums, third_beside, third_over = stage(
+        (own_sums, far_sums, other_sums, third_beside, third_over)
+    )
+    third_over_swapped, third_beside_swapped = core_swap(third_over), core_swap(third_beside)
+    far_sums, other_sums = add_sums([third_over, third_beside], (far_sums, far, 0, 1), (other_sums, other, 1, 2))
     far_sums, other_sums = add_sums(
-        [third_over, third_beside], (far_sums, far, 0, 1), (other_sums, other, 1, 2)
-    )
-    far_total = far_sums[0] + core_swap(far_sums[1])
-    other_total = other_sums[0] + core_swap(other_sums[1])
-
-    far_total, other_total, own_sums = stage((far_total, other_total, own_sums))
-    far_returned = column_swap(far_total)
-    (other_returned,) = over_members(other_total)
-    (own_sums,) = add_sums([near_beside, second_over, third, third_over, third_beside], (own_sums, own, 0, 5))
-    swapped = core_swap_parts(own_sums[1])
-    return (own_sums[0] + swapped + far_returned + other_returned) * math.exp(-2.0)
+        [third_over_swapped, third_beside_swapped], (far_sums, far, 0, 1), (other_sums, other, 1, 2)
+    )
+    own_sums, other_sums, far_sums = stage((own_sums, other_sums, far_sums))
+    far_returned = column_swap(far_sums[0])
+    (other_returned,) = over_members(other_sums[0])
+    rest = [second, second_swapped, near_beside, near_beside_swapped, second_over, second_over_swapped, third, third_swapped, third_over, third_over_swapped, third_beside, third_beside_swapped]
+    (own_sums,) = add_sums(rest, (own_sums, own, 0, len(rest)))
+    return (own_sums[0] + far_returned + other_returned) * math.exp(-2.0)
 
 
 def local(embeddings):

time: 75.9 us -> 75.6 us (level)
  local copies, waits for them, and re-layouts: 5.15 us -> 1.43 us
  waiting for transfers between devices: 19.9 us -> 23.2 us
    ppermute x17 -> x18, waiting for transfers between devices: 19.9 us -> 23.2 us  [moved(): lax.ppermute(value, axis, [pair for pair in pairs if pair[1] is not None])]
    dynamic_slice x2 -> x1, local copies, waits for them, and re-layouts: 3.33 us -> 1.36 us  [half(): return lax.dynamic_slice_in_dim(block, index * share, share)]
    unnamed x17 -> x2, local copies, waits for them, and re-layouts: 1 us -> 0.01 us
    split x2 -> x0, local copies, waits for them, and re-layouts: 0.76 us -> none  [core_swap_parts(): return jnp.concatenate([core_swap(rows) for rows in jnp.split(value, 2)])]
    ppermute x17 -> x18, starting transfers between devices: 16.9 us -> 17.1 us  [moved(): lax.ppermute(value, axis, [pair for pair in pairs if pair[1] is not None])]
  transfers between devices with their start and end apart: 17 -> 18, of which waited for: 10 -> 9; matrix products, arithmetic and copies ran while one was open for 7% -> 2% of each run, Pallas kernels for 40% -> 41%
where the time goes in v2:
time: 75.6 us; the launch traced here: 75.4 us
  Pallas kernels  32.6 us (43%)
  waiting for transfers between devices  23.2 us (31%)
  starting transfers between devices  17.1 us (23%)
  local copies, waits for them, and re-layouts  1.43 us (2%)
  other arithmetic  0.96 us (1%)
    pallas_call x6, Pallas kernels, add_sums(): pl.pallas_call(functools.partial(sums_kernel, jobs=plan, n_pieces=len(pie...  32.6 us
    ppermute x18, waiting for transfers between devices, moved(): lax.ppermute(value, axis, [pair for pair in pairs if pair[1] is not None])  23.2 us
    ppermute x18, starting transfers between devices, moved(): lax.ppermute(value, axis, [pair for pair in pairs if pair[1] is not None])  17.1 us
  transfers between devices with their start and end apart: 18, of which 9 were waited for; matrix products, arithmetic and copies ran while one was open for 2% of the time, Pallas kernels for 41%

profile of v2, /device:TPU:0, one launch (start us, length us, event | category | flops | bytes accessed | tf_op | source)
XLA Modules:
  0.0 75.4 jit_solution(16547027669422360133)
XLA Ops:
  0.5 1.4 %constant_dynamic-slice_fusion = (f32[512,256]{1,0:T(8,128)S(1)}, f32[512,256]{1,0:T(8,128)S(1)}) fusion(f32[1024,256]{1,0:T(8,128)} %refs_0_.3, s32[]{:T(128)S(6)} %select_n.20, s32[]{:T(128)S(6)} %select_n.19), kind=kLoop, calls=%fused_computation.2 | loop fusion | bytes 2097160 | tf_op jit(solution)/shard_map/dynamic_slice | solution.py:169
  1.8 4.7 %collective-permute-start = (f32[512,256]{1,0:T(8,128)S(1)}, f32[512,256]{1,0:T(8,128)S(1)}, u32[]{:S(2)}, u32[]{:S(2)}) collective-permute-start(f32[512,256]{1,0:T(8,128)S(1)} %get-tuple-element.56.refs_2_.refs_8_.refs_12_), channel_id=1, source_target_pairs={{0,24},{2,26},{4,28},{6,30},{8,16},{10,18},{12,20},{14,22},{16,8},... | collective-permute-start | bytes 1572872 | tf_op jit(solution)/shard_map/ppermute | solution.py:18
  6.5 1.5 %collective-permute-start.2 = (f32[512,256]{1,0:T(8,128)S(1)}, f32[512,256]{1,0:T(8,128)S(1)}, u32[]{:S(2)}, u32[]{:S(2)}) collective-permute-start(f32[512,256]{1,0:T(8,128)S(1)} %get-tuple-element.56.refs_2_.refs_8_.refs_12_), channel_id=1, source_target_pairs={{0,4},{2,6},{4,0},{6,2},{8,12},{10,14},{12,8},{14,10},{16,20},{18,... | collective-permute-start | bytes 1572872 | tf_op jit(solution)/shard_map/ppermute | solution.py:18
  8.0 5.1 %shard_map.17.refs_9_ = f32[512,256]{1,0:T(8,128)S(1)} custom-call(f32[1024,256]{1,0:T(8,128)S(1)} %copy-done, f32[1024,256]{1,0:T(8,128)} %collective-permute-done.3.refs_1_, f32[512,256]{1,0:T(8,128)S(1)} %get-tuple-element.56.refs_2_.refs_8_.refs_12_), custom_call_target="tpu_custom_call" | custom-call | flops 1 | bytes 1 | tf_op jit(solution)/shard_map/pallas_call | solution.py:151
  13.0 6.3 %collective-permute-done.refs_2_.refs_0_ = f32[512,256]{1,0:T(8,128)S(1)} collective-permute-done((f32[512,256]{1,0:T(8,128)S(1)}, f32[512,256]{1,0:T(8,128)S(1)}, u32[]{:S(2)}, u32[]{:S(2)}) %collective-permute-start) | collective-permute-done | bytes 524320 | tf_op jit(solution)/shard_map/ppermute | solution.py:18
  19.3 11.2 %collective-permute-done.1.refs_4_ = f32[512,256]{1,0:T(8,128)} collective-permute-done((f32[512,256]{1,0:T(8,128)S(1)}, f32[512,256]{1,0:T(8,128)}, u32[]{:S(2)}, u32[]{:S(2)}) %collective-permute-start.1) | collective-permute-done | bytes 524320 | tf_op jit(solution)/shard_map/ppermute | solution.py:18
  31.1 0.8 %collective-permute-start.10 = (f32[512,256]{1,0:T(8,128)S(1)}, f32[512,256]{1,0:T(8,128)S(1)}, u32[]{:S(2)}, u32[]{:S(2)}) collective-permute-start(f32[512,256]{1,0:T(8,128)S(1)} %broadcast_select_fusion), channel_id=1, source_target_pairs={{0,16},{2,18},{4,20},{6,22},{8,0},{10,2},{12,4},{14,6},{16,24},{18... | collective-permute-start | bytes 1572872 | tf_op jit(solution)/shard_map/ppermute | solution.py:18
  31.9 1.5 %collective-permute-start.5 = (f32[512,256]{1,0:T(8,128)}, f32[512,256]{1,0:T(8,128)S(1)}, u32[]{:S(2)}, u32[]{:S(2)}) collective-permute-start(f32[512,256]{1,0:T(8,128)} %collective-permute-done.1.refs_4_), channel_id=1, source_target_pairs={{0,4},{2,6},{4,0},{6,2},{8,12},{10,14},{12,8},{14,10},{16,20},{18,... | collective-permute-start | bytes 1572872 | tf_op jit(solution)/shard_map/ppermute | solution.py:18
  33.4 1.5 %collective-permute-start.7 = (f32[512,256]{1,0:T(8,128)S(1)}, f32[512,256]{1,0:T(8,128)S(1)}, u32[]{:S(2)}, u32[]{:S(2)}) collective-permute-start(f32[512,256]{1,0:T(8,128)S(1)} %collective-permute-done.refs_2_.refs_0_), channel_id=1, source_target_pairs={{0,1},{1,0},{2,3},{3,2},{4,5},{5,4},{6,7},{7,6},{8,9},{9,8},{10,11... | collective-permute-start | bytes 1572872 | tf_op jit(solution)/shard_map/ppermute | solution.py:18
  34.9 10.1 %shard_map.18 = (f32[512,256]{1,0:T(8,128)S(1)}, f32[512,256]{1,0:T(8,128)S(1)}, f32[512,256]{1,0:T(8,128)S(1)}) custom-call(f32[1024,256]{1,0:T(8,128)S(1)} %copy-done, f32[1024,256]{1,0:T(8,128)} %collective-permute-done.3.refs_1_, f32[512,256]{1,0:T(8,128)S(1)} %collective-permute-done.refs_2_.refs_0_, ...), custom_call_target="tpu_custom_call" | custom-call | flops 1 | bytes 1 | tf_op jit(solution)/shard_map/pallas_call | solution.py:151
  45.2 0.5 collective-permute-done.5.refs_0_.refs_2_
  45.7 1.0 %collective-permute-done.7.refs_6_.refs_4_ = f32[512,256]{1,0:T(8,128)S(1)} collective-permute-done((f32[512,256]{1,0:T(8,128)S(1)}, f32[512,256]{1,0:T(8,128)S(1)}, u32[]{:S(2)}, u32[]{:S(2)}) %collective-permute-start.7) | collective-permute-done | bytes 524320 | tf_op jit(solution)/shard_map/ppermute | solution.py:18
  46.7 1.1 %collective-permute-start.12 = (f32[256,256]{1,0:T(8,128)S(1)}, f32[256,256]{1,0:T(8,128)S(1)}, u32[]{:S(2)}, u32[]{:S(2)}) collective-permute-start(f32[256,256]{1,0:T(8,128)S(1)} %get-tuple-element.60.refs_2_), channel_id=1, source_target_pairs={{0,4},{2,6},{4,0},{6,2},{8,12},{10,14},{12,8},{14,10},{16,20},{18,... | collective-permute-start | bytes 786440 | tf_op jit(solution)/shard_map/ppermute | solution.py:18
  47.8 1.5 %collective-permute-start.13 = (f32[256,256]{1,0:T(8,128)S(1)}, f32[256,256]{1,0:T(8,128)S(1)}, u32[]{:S(2)}, u32[]{:S(2)}) collective-permute-start(f32[256,256]{1,0:T(8,128)S(1)} %get-tuple-element.59.refs_4_), channel_id=1, source_target_pairs={{0,1},{1,0},{2,3},{3,2},{4,5},{5,4},{6,7},{7,6},{8,9},{9,8},{10,11... | collective-permute-start | bytes 786440 | tf_op jit(solution)/shard_map/ppermute | solution.py:18
  49.4 5.7 %shard_map.19 = (f32[512,256]{1,0:T(8,128)S(1)}, f32[512,256]{1,0:T(8,128)S(1)}) custom-call(f32[512,256]{1,0:T(8,128)S(1)} %collective-permute-done.5.refs_0_.refs_2_, f32[512,256]{1,0:T(8,128)S(1)} %collective-permute-done.6.refs_1_.refs_3_, f32[256,256]{1,0:T(8,128)S(1)} %get-tuple-element.60.refs_2_, f32[256,256]{1,0:T(8,128)S(1)} %get-tuple-element.58.refs_3_, ...), custom_call_target="tpu_custom_call" | custom-call | flops 1 | bytes 1 | tf_op jit(solution)/shard_map/pallas_call | solution.py:151
  55.8 0.5 collective-permute-start.15
  56.3 1.5 %shard_map.20 = (f32[512,256]{1,0:T(8,128)S(1)}, f32[512,256]{1,0:T(8,128)S(1)}) custom-call(f32[256,256]{1,0:T(8,128)S(1)} %collective-permute-done.13.refs_0_.refs_8_, f32[256,256]{1,0:T(8,128)S(1)} %collective-permute-done.12.refs_1_.refs_10_, f32[512,256]{1,0:T(8,128)S(1)} %collective-permute-done.2.refs_6_.refs_9_.refs_2_, ...), custom_call_target="tpu_custom_call" | custom-call | flops 1 | bytes 1 | tf_op jit(solution)/shard_map/pallas_call | solution.py:151
  57.8 1.5 %shard_map.21 = (f32[512,256]{1,0:T(8,128)S(1)}, f32[512,256]{1,0:T(8,128)S(1)}) custom-call(f32[256,256]{1,0:T(8,128)S(1)} %collective-permute-done.14.refs_0_.refs_9_, f32[256,256]{1,0:T(8,128)S(1)} %collective-permute-done.15.refs_1_.refs_11_, f32[512,256]{1,0:T(8,128)S(1)} %collective-permute-done.2.refs_6_.refs_9_.refs_2_, ...), custom_call_target="tpu_custom_call" | custom-call | flops 1 | bytes 1 | tf_op jit(solution)/shard_map/pallas_call | solution.py:151
  59.3 1.6 %collective-permute-start.17 = (f32[512,256]{1,0:T(8,128)S(1)}, f32[512,256]{1,0:T(8,128)S(1)}, u32[]{:S(2)}, u32[]{:S(2)}) collective-permute-start(f32[512,256]{1,0:T(8,128)S(1)} %get-tuple-element.54), channel_id=1, source_target_pairs={{0,1},{1,0},{2,3},{3,2},{4,5},{5,4},{6,7},{7,6},{8,9},{9,8},{10,11... | collective-permute-start | bytes 1572872 | tf_op jit(solution)/shard_map/ppermute | solution.py:18
  60.9 1.5 %collective-permute-start.16 = (f32[512,256]{1,0:T(8,128)S(1)}, f32[512,256]{1,0:T(8,128)S(1)}, u32[]{:S(2)}, u32[]{:S(2)}) collective-permute-start(f32[512,256]{1,0:T(8,128)S(1)} %get-tuple-element.53), channel_id=1, source_target_pairs={{0,4},{2,6},{4,0},{6,2},{8,12},{10,14},{12,8},{14,10},{16,20},{18,... | collective-permute-start | bytes 1572872 | tf_op jit(solution)/shard_map/ppermute | solution.py:18
  62.4 8.7 %shard_map.22 = f32[512,256]{1,0:T(8,128)S(1)} custom-call(f32[512,256]{1,0:T(8,128)S(1)} %collective-permute-done.refs_2_.refs_0_, f32[512,256]{1,0:T(8,128)S(1)} %collective-permute-done.4.refs_3_.refs_1_, f32[512,256]{1,0:T(8,128)S(1)} %collective-permute-done.5.refs_0_.refs_2_, f32[512,256]{1,0:T(8,128)S(1)} %collective-permute-done.6.refs_1_.refs_3_, ...), custom_call_target="tpu_custom_call" | custom-call | flops 1 | bytes 1 | tf_op jit(solution)/shard_map/pallas_call | solution.py:151
  71.2 2.1 %collective-permute-done.17 = f32[512,256]{1,0:T(8,128)S(1)} collective-permute-done((f32[512,256]{1,0:T(8,128)S(1)}, f32[512,256]{1,0:T(8,128)S(1)}, u32[]{:S(2)}, u32[]{:S(2)}) %collective-permute-start.17) | collective-permute-done | bytes 524320 | tf_op jit(solution)/shard_map/ppermute | solution.py:18
  73.2 1.2 %collective-permute-done.16 = f32[512,256]{1,0:T(8,128)S(1)} collective-permute-done((f32[512,256]{1,0:T(8,128)S(1)}, f32[512,256]{1,0:T(8,128)S(1)}, u32[]{:S(2)}, u32[]{:S(2)}) %collective-permute-start.16) | collective-permute-done | bytes 524320 | tf_op jit(solution)/shard_map/ppermute | solution.py:18
  74.5 0.9 %add_multiply_fusion = f32[512,256]{1,0:T(8,128)} fusion(f32[512,256]{1,0:T(8,128)S(1)} %collective-permute-done.17, f32[512,256]{1,0:T(8,128)S(1)} %shard_map.22, f32[512,256]{1,0:T(8,128)S(1)} %collective-permute-done.16), kind=kLoop, calls=%fused_computation | loop fusion | flops 393216 | bytes 2097152 | tf_op jit(solution)/shard_map/mul | solution.py:238
  (25 shorter events, 2.0 us)
Async XLA Ops:
  0.0 8.0 %collective-permute-start.3 = (f32[1024,256]{1,0:T(8,128)}, f32[1024,256]{1,0:T(8,128)}, u32[]{:S(2)}, u32[]{:S(2)}) collective-permute-start(f32[1024,256]{1,0:T(8,128)} %refs_0_.3), channel_id=1, source_target_pairs={{0,2},{2,0},{4,6},{6,4},{8,10},{10,8},{12,14},{14,12},{16,18},{18,... | collective-permute-start | bytes 3145736 | tf_op jit(solution)/shard_map/ppermute | solution.py:18
  0.5 7.5 %copy-start = (f32[1024,256]{1,0:T(8,128)S(1)}, f32[1024,256]{1,0:T(8,128)}, u32[]{:S(2)}) copy-start(f32[1024,256]{1,0:T(8,128)} %refs_0_.3) | copy-start | bytes 3145732
  1.8 17.5 %collective-permute-start = (f32[512,256]{1,0:T(8,128)S(1)}, f32[512,256]{1,0:T(8,128)S(1)}, u32[]{:S(2)}, u32[]{:S(2)}) collective-permute-start(f32[512,256]{1,0:T(8,128)S(1)} %get-tuple-element.56.refs_2_.refs_8_.refs_12_), channel_id=1, source_target_pairs={{0,24},{2,26},{4,28},{6,30},{8,16},{10,18},{12,20},{14,22},{16,8},... | collective-permute-start | bytes 1572872 | tf_op jit(solution)/shard_map/ppermute | solution.py:18
  6.5 24.0 %collective-permute-start.1 = (f32[512,256]{1,0:T(8,128)S(1)}, f32[512,256]{1,0:T(8,128)}, u32[]{:S(2)}, u32[]{:S(2)}) collective-permute-start(f32[512,256]{1,0:T(8,128)S(1)} %get-tuple-element.56.refs_2_.refs_8_.refs_12_), channel_id=1, source_target_pairs={{0,8},{2,10},{4,12},{6,14},{8,0},{10,2},{12,4},{14,6},{16,24},{18,... | collective-permute-start | bytes 1572872 | tf_op jit(solution)/shard_map/ppermute | solution.py:18
  6.5 24.0 %collective-permute-start.2 = (f32[512,256]{1,0:T(8,128)S(1)}, f32[512,256]{1,0:T(8,128)S(1)}, u32[]{:S(2)}, u32[]{:S(2)}) collective-permute-start(f32[512,256]{1,0:T(8,128)S(1)} %get-tuple-element.56.refs_2_.refs_8_.refs_12_), channel_id=1, source_target_pairs={{0,4},{2,6},{4,0},{6,2},{8,12},{10,14},{12,8},{14,10},{16,20},{18,... | collective-permute-start | bytes 1572872 | tf_op jit(solution)/shard_map/ppermute | solution.py:18
  30.5 4.4 %collective-permute-start.4 = (f32[512,256]{1,0:T(8,128)S(1)}, f32[512,256]{1,0:T(8,128)S(1)}, u32[]{:S(2)}, u32[]{:S(2)}) collective-permute-start(f32[512,256]{1,0:T(8,128)S(1)} %collective-permute-done.refs_2_.refs_0_), channel_id=1, source_target_pairs={{0,2},{2,0},{4,6},{6,4},{8,10},{10,8},{12,14},{14,12},{16,18},{18,... | collective-permute-start | bytes 1572872 | tf_op jit(solution)/shard_map/ppermute | solution.py:18
  30.6 4.3 %collective-permute-start.9 = (f32[512,256]{1,0:T(8,128)}, f32[512,256]{1,0:T(8,128)S(1)}, u32[]{:S(2)}, u32[]{:S(2)}) collective-permute-start(f32[512,256]{1,0:T(8,128)} %collective-permute-done.1.refs_4_), channel_id=1, source_target_pairs={{0,2},{2,0},{4,6},{6,4},{8,10},{10,8},{12,14},{14,12},{16,18},{18,... | collective-permute-start | bytes 1572872 | tf_op jit(solution)/shard_map/ppermute | solution.py:18
  31.1 14.1 %collective-permute-start.10 = (f32[512,256]{1,0:T(8,128)S(1)}, f32[512,256]{1,0:T(8,128)S(1)}, u32[]{:S(2)}, u32[]{:S(2)}) collective-permute-start(f32[512,256]{1,0:T(8,128)S(1)} %broadcast_select_fusion), channel_id=1, source_target_pairs={{0,16},{2,18},{4,20},{6,22},{8,0},{10,2},{12,4},{14,6},{16,24},{18... | collective-permute-start | bytes 1572872 | tf_op jit(solution)/shard_map/ppermute | solution.py:18
  31.9 13.8 %collective-permute-start.5 = (f32[512,256]{1,0:T(8,128)}, f32[512,256]{1,0:T(8,128)S(1)}, u32[]{:S(2)}, u32[]{:S(2)}) collective-permute-start(f32[512,256]{1,0:T(8,128)} %collective-permute-done.1.refs_4_), channel_id=1, source_target_pairs={{0,4},{2,6},{4,0},{6,2},{8,12},{10,14},{12,8},{14,10},{16,20},{18,... | collective-permute-start | bytes 1572872 | tf_op jit(solution)/shard_map/ppermute | solution.py:18
  33.4 13.3 %collective-permute-start.7 = (f32[512,256]{1,0:T(8,128)S(1)}, f32[512,256]{1,0:T(8,128)S(1)}, u32[]{:S(2)}, u32[]{:S(2)}) collective-permute-start(f32[512,256]{1,0:T(8,128)S(1)} %collective-permute-done.refs_2_.refs_0_), channel_id=1, source_target_pairs={{0,1},{1,0},{2,3},{3,2},{4,5},{5,4},{6,7},{7,6},{8,9},{9,8},{10,11... | collective-permute-start | bytes 1572872 | tf_op jit(solution)/shard_map/ppermute | solution.py:18
  45.2 4.1 %collective-permute-start.11 = (f32[512,256]{1,0:T(8,128)S(1)}, f32[512,256]{1,0:T(8,128)S(1)}, u32[]{:S(2)}, u32[]{:S(2)}) collective-permute-start(f32[512,256]{1,0:T(8,128)S(1)} %collective-permute-done.10.refs_6_), channel_id=1, source_target_pairs={{0,2},{2,0},{4,6},{6,4},{8,10},{10,8},{12,14},{14,12},{16,18},{18,... | collective-permute-start | bytes 1572872 | tf_op jit(solution)/shard_map/ppermute | solution.py:18
  45.7 3.7 %collective-permute-start.6 = (f32[512,256]{1,0:T(8,128)S(1)}, f32[512,256]{1,0:T(8,128)S(1)}, u32[]{:S(2)}, u32[]{:S(2)}) collective-permute-start(f32[512,256]{1,0:T(8,128)S(1)} %collective-permute-done.5.refs_0_.refs_2_), channel_id=1, source_target_pairs={{0,2},{2,0},{4,6},{6,4},{8,10},{10,8},{12,14},{14,12},{16,18},{18,... | collective-permute-start | bytes 1572872 | tf_op jit(solution)/shard_map/ppermute | solution.py:18
  46.7 2.7 %collective-permute-start.8 = (f32[512,256]{1,0:T(8,128)S(1)}, f32[512,256]{1,0:T(8,128)S(1)}, u32[]{:S(2)}, u32[]{:S(2)}) collective-permute-start(f32[512,256]{1,0:T(8,128)S(1)} %collective-permute-done.7.refs_6_.refs_4_), channel_id=1, source_target_pairs={{0,2},{2,0},{4,6},{6,4},{8,10},{10,8},{12,14},{14,12},{16,18},{18,... | collective-permute-start | bytes 1572872 | tf_op jit(solution)/shard_map/ppermute | solution.py:18
  46.7 8.8 %collective-permute-start.12 = (f32[256,256]{1,0:T(8,128)S(1)}, f32[256,256]{1,0:T(8,128)S(1)}, u32[]{:S(2)}, u32[]{:S(2)}) collective-permute-start(f32[256,256]{1,0:T(8,128)S(1)} %get-tuple-element.60.refs_2_), channel_id=1, source_target_pairs={{0,4},{2,6},{4,0},{6,2},{8,12},{10,14},{12,8},{14,10},{16,20},{18,... | collective-permute-start | bytes 786440 | tf_op jit(solution)/shard_map/ppermute | solution.py:18
  47.8 8.0 %collective-permute-start.13 = (f32[256,256]{1,0:T(8,128)S(1)}, f32[256,256]{1,0:T(8,128)S(1)}, u32[]{:S(2)}, u32[]{:S(2)}) collective-permute-start(f32[256,256]{1,0:T(8,128)S(1)} %get-tuple-element.59.refs_4_), channel_id=1, source_target_pairs={{0,1},{1,0},{2,3},{3,2},{4,5},{5,4},{6,7},{7,6},{8,9},{9,8},{10,11... | collective-permute-start | bytes 786440 | tf_op jit(solution)/shard_map/ppermute | solution.py:18
  55.8 2.0 %collective-permute-start.14 = (f32[256,256]{1,0:T(8,128)S(1)}, f32[256,256]{1,0:T(8,128)S(1)}, u32[]{:S(2)}, u32[]{:S(2)}) collective-permute-start(f32[256,256]{1,0:T(8,128)S(1)} %collective-permute-done.13.refs_0_.refs_8_), channel_id=1, source_target_pairs={{0,2},{2,0},{4,6},{6,4},{8,10},{10,8},{12,14},{14,12},{16,18},{18,... | collective-permute-start | bytes 786440 | tf_op jit(solution)/shard_map/ppermute | solution.py:18
  55.8 2.0 %collective-permute-start.15 = (f32[256,256]{1,0:T(8,128)S(1)}, f32[256,256]{1,0:T(8,128)S(1)}, u32[]{:S(2)}, u32[]{:S(2)}) collective-permute-start(f32[256,256]{1,0:T(8,128)S(1)} %collective-permute-done.12.refs_1_.refs_10_), channel_id=1, source_target_pairs={{0,2},{2,0},{4,6},{6,4},{8,10},{10,8},{12,14},{14,12},{16,18},{18,... | collective-permute-start | bytes 786440 | tf_op jit(solution)/shard_map/ppermute | solution.py:18
  59.3 13.9 %collective-permute-start.17 = (f32[512,256]{1,0:T(8,128)S(1)}, f32[512,256]{1,0:T(8,128)S(1)}, u32[]{:S(2)}, u32[]{:S(2)}) collective-permute-start(f32[512,256]{1,0:T(8,128)S(1)} %get-tuple-element.54), channel_id=1, source_target_pairs={{0,1},{1,0},{2,3},{3,2},{4,5},{5,4},{6,7},{7,6},{8,9},{9,8},{10,11... | collective-permute-start | bytes 1572872 | tf_op jit(solution)/shard_map/ppermute | solution.py:18
  60.9 13.6 %collective-permute-start.16 = (f32[512,256]{1,0:T(8,128)S(1)}, f32[512,256]{1,0:T(8,128)S(1)}, u32[]{:S(2)}, u32[]{:S(2)}) collective-permute-start(f32[512,256]{1,0:T(8,128)S(1)} %get-tuple-element.53), channel_id=1, source_target_pairs={{0,4},{2,6},{4,0},{6,2},{8,12},{10,14},{12,8},{14,10},{16,20},{18,... | collective-permute-start | bytes 1572872 | tf_op jit(solution)/shard_map/ppermute | solution.py:18
